TPU v7x, 512 devices: a whole 4x4x16 slice. The times are simulated.
512 devices in a mesh: pipe: 8 (over x_hi, y), expert: 64 (over z, x_lo, core).
Axes of the slice: x: 4 (x_hi: 2, x_lo: 2; x = x_hi * 2 + x_lo), y: 4, z: 16, core: 2. Of those that a mesh axis runs over, the one named last changes fastest.
Arguments:
- fwd_input: bfloat16 [8, 4096, 3584], P('pipe', 'expert'), may hold values from -6 to 6
- fwd_cotangent: bfloat16 [8, 4096, 3584], P('pipe', 'expert'), may hold values from -6 to 6
- rev_input: bfloat16 [8, 4096, 3584], P('pipe', 'expert'), may hold values from -6 to 6
- rev_cotangent: bfloat16 [8, 4096, 3584], P('pipe', 'expert'), may hold values from -6 to 6
- fwd_routes: int32 [8, 4096, 8], P('pipe', 'expert'), may hold values from 0 to 255, all different within a row; in each aligned block of 64 rows (0 to 63, 64 to 127, ..., all dimensions but the last counted through in order) at most 5 rows name the same one
- rev_routes: int32 [8, 4096, 8], P('pipe', 'expert'), may hold values from 0 to 255, all different within a row; in each aligned block of 64 rows (0 to 63, 64 to 127, ..., all dimensions but the last counted through in order) at most 5 rows name the same one
- fwd_scores: float32 [8, 4096, 8], P('pipe', 'expert'), may hold values from 0.05 to 1
- rev_scores: float32 [8, 4096, 8], P('pipe', 'expert'), may hold values from 0.05 to 1
- norm_gain: float32 [8, 3584], P('pipe'), may hold values from 0.5 to 1.5
- w_gate: bfloat16 [8, 3584, 8192], P('pipe', None, 'expert'), may hold values from -0.09375 to 0.09375
- w_up: bfloat16 [8, 3584, 8192], P('pipe', None, 'expert'), may hold values from -0.09375 to 0.09375
Outputs:
- grad_down: bfloat16 [8, 8192, 3584], P('pipe', 'expert')
Inputs may be any that keep to these rules, and one draw needn't show every extreme that they name: `fwd_routes`: in the rows of one device of a micro-batch and group (aligned blocks of 64 rows) no expert is chosen by more than 5 rows; a token's 8 experts differ. `rev_routes`: as fwd_routes.
All inputs are finite; a program needn't handle non-finite values.
Results may differ from a plain program's by a relative error of at most 0.0076.
Values may be sent and summed in bfloat16 or wider, within the bound.
A program may use at most 128 MiB of HBM per device.

v0:
```python
import jax
import jax.numpy as jnp
from jax import lax
from jax.sharding import PartitionSpec as P

FF = 2048
CAP = 5


def swapped(value, axis, stride):
    return lax.ppermute(value, axis, [(i, i ^ 1 << stride) for i in range(lax.axis_size(axis))])


def route_weights(routes, scores, experts):
    total = jnp.sum(scores, axis=-1, keepdims=True)
    share = 2.5 * scores / total
    hits = (routes[..., None] == jnp.arange(experts, dtype=jnp.int32)).astype(jnp.float32)
    return jnp.sum(hits * share[..., None], axis=-2).astype(jnp.bfloat16)


def norm_rows(tokens, gain):
    values = tokens.astype(jnp.float32)
    return (
        values * lax.rsqrt(jnp.mean(values * values, axis=-1, keepdims=True) + 1e-06) * gain
    ).astype(jnp.bfloat16)


def scale_rows(cotangent, weights):
    return (weights.T.astype(jnp.float32)[:, :, None] * cotangent.astype(jnp.float32)[None]).astype(
        jnp.bfloat16
    )


def slot_select(weights, capacity):
    taken = (weights.T > 0).astype(jnp.int32)
    place = jnp.cumsum(taken, axis=1) - 1
    slots = jnp.arange(capacity, dtype=jnp.int32)
    return ((place[:, None, :] == slots[None, :, None]) & (taken[:, None, :] == 1)).astype(
        jnp.bfloat16
    )


def pack_rows(tokens, cotangent, weights, gain, capacity):
    select = slot_select(weights, capacity)
    normed = norm_rows(tokens, gain)
    scaled = scale_rows(cotangent, weights)
    rows = jnp.einsum("ept,td->epd", select, normed, preferred_element_type=jnp.float32).astype(
        jnp.bfloat16
    )
    grads = jnp.einsum("ept,etd->epd", select, scaled, preferred_element_type=jnp.float32).astype(
        jnp.bfloat16
    )
    return (rows, grads)


def body(
    fwd_input,
    fwd_cotangent,
    rev_input,
    rev_cotangent,
    fwd_routes,
    rev_routes,
    fwd_scores,
    rev_scores,
    norm_gain,
    w_gate,
    w_up,
):
    n_expert = lax.axis_size("expert")
    width = w_gate.shape[2]
    pieces = FF // width
    experts = n_expert // pieces
    gain = norm_gain[0]
    fwd_weights = route_weights(fwd_routes[0], fwd_scores[0], experts)
    fwd_rows, fwd_grads = pack_rows(fwd_input[0], fwd_cotangent[0], fwd_weights, gain, CAP)
    rev_weights = route_weights(rev_routes[0], rev_scores[0], experts)
    moving = (rev_input, rev_cotangent, rev_weights[None])
    for bit in range(lax.axis_size("pipe").bit_length() - 1):
        moving = swapped((moving[0], moving[1], moving[2]), "pipe", bit)
    arrived = tuple((member[0] for member in moving))
    rev_rows, rev_grads = pack_rows(arrived[0], arrived[1], arrived[2], gain, CAP)
    joined_rows = jnp.repeat(jnp.concatenate([fwd_rows, rev_rows], axis=1), pieces, axis=0)
    joined_grads = jnp.repeat(jnp.concatenate([fwd_grads, rev_grads], axis=1), pieces, axis=0)
    received, received_grads = (
        lax.all_to_all(joined_rows, "expert", split_axis=0, concat_axis=0, tiled=True),
        lax.all_to_all(joined_grads, "expert", split_axis=0, concat_axis=0, tiled=True),
    )
    features = received.shape[-1]
    flat_rows = received.reshape(-1, features)
    flat_grads = received_grads.reshape(-1, features)
    gate = jnp.dot(flat_rows, w_gate[0], preferred_element_type=jnp.float32)
    up = jnp.dot(flat_rows, w_up[0], preferred_element_type=jnp.float32)
    hidden = (jax.nn.silu(gate) * up).astype(jnp.bfloat16)
    grad = lax.dot_general(
        hidden, flat_grads, (((0,), (0,)), ((), ())), preferred_element_type=jnp.float32
    )
    return grad.astype(jnp.bfloat16)[None]


def solution(mesh):
    in_specs = (
        P("pipe", "expert", None),
        P("pipe", "expert", None),
        P("pipe", "expert", None),
        P("pipe", "expert", None),
        P("pipe", "expert", None),
        P("pipe", "expert", None),
        P("pipe", "expert", None),
        P("pipe", "expert", None),
        P("pipe", None),
        P("pipe", None, "expert"),
        P("pipe", None, "expert"),
    )
    out_specs = P("pipe", "expert", None)
    return jax.shard_map(body, mesh=mesh, in_specs=in_specs, out_specs=out_specs, check_vma=False)
```

profile of v0, /device:TPU:1, one launch (start us, length us, event | category | flops | bytes accessed | tf_op | source)
XLA Modules:
  0.0 740.5 jit_solution(5967818785870707171)
XLA Ops:
  0.0 0.8 reduce_sum.57
  0.8 0.7 bitcast_divide_fusion
  1.5 0.7 select_reduce_fusion
  2.2 4.0 collective-permute-start
  6.2 1.9 collective-permute-start.3
  8.2 0.7 reduce_sum.54
  8.9 0.7 bitcast_divide_fusion.1
  9.6 0.7 select_reduce_fusion.1
  10.3 0.2 reduce_window_sum.17
  10.5 1.2 fusion.6
  11.7 0.0 collective-permute-done
  11.8 5.0 collective-permute-start.1
  16.7 0.0 collective-permute-done.3
  16.8 7.2 collective-permute-start.4
  23.9 0.8 reduce.2
  24.7 0.0 collective-permute-done.1
  24.7 4.7 collective-permute-start.2
  29.4 1.3 convolution_convert_fusion.4
  30.7 1.3 collective-permute-done.4
  31.9 5.6 collective-permute-start.5
  37.6 0.0 collective-permute-done.2
  37.6 0.2 reduce_window_sum.18
  37.9 7.6 %collective-permute-done.5 = bf16[1,64,3584]{2,1,0:T(8,128)(2,1)S(1)} collective-permute-done((bf16[1,64,3584]{2,1,0:T(8,128)(2,1)S(1)}, bf16[1,64,3584]{2,1,0:T(8,128)(2,1)S(1)}, u32[]{:S(2)}, u32[]{:S(2)}) %collective-permute-start.5) | collective-permute-done | bytes 458784 | tf_op jit(solution)/shard_map/ppermute | solution.py:11
  45.4 0.2 fusion.9
  45.6 0.3 convolution_convert_fusion.3
  45.9 0.2 pad_maximum_fusion
  46.1 3.9 broadcast_in_dim.6
  50.0 20.7 %all-to-all-start = ((bf16[64,10,3584]{2,1,0:T(8,128)(2,1)}), bf16[64,10,3584]{2,1,0:T(8,128)(2,1)}, u32[]{:S(2)}, u32[]{:S(2)}) async-start(bf16[64,10,3584]{2,1,0:T(8,128)(2,1)} %bitcast.67), calls=%async_computation | async-start | bytes 14680064 | tf_op jit(solution)/shard_map/all_to_all | solution.py:85
  70.7 2.1 collective-permute-start.6
  72.8 11.5 %collective-permute-done.6 = bf16[1,64,3584]{2,1,0:T(8,128)(2,1)S(1)} collective-permute-done((bf16[1,64,3584]{2,1,0:T(8,128)(2,1)S(1)}, bf16[1,64,3584]{2,1,0:T(8,128)(2,1)S(1)}, u32[]{:S(2)}, u32[]{:S(2)}) %collective-permute-start.6) | collective-permute-done | bytes 458784 | tf_op jit(solution)/shard_map/ppermute | solution.py:11
  84.3 4.5 collective-permute-start.7
  88.8 0.1 bitcast_convert_fusion.1
  88.9 9.6 %collective-permute-done.7 = bf16[1,64,3584]{2,1,0:T(8,128)(2,1)S(1)} collective-permute-done((bf16[1,64,3584]{2,1,0:T(8,128)(2,1)S(1)}, bf16[1,64,3584]{2,1,0:T(8,128)(2,1)S(1)}, u32[]{:S(2)}, u32[]{:S(2)}) %collective-permute-start.7) | collective-permute-done | bytes 458784 | tf_op jit(solution)/shard_map/ppermute | solution.py:11
  98.5 4.3 collective-permute-start.8
  102.9 0.4 convolution_convert_fusion.2
  103.3 11.2 %collective-permute-done.8 = bf16[1,64,3584]{2,1,0:T(8,128)(2,1)S(1)} collective-permute-done((bf16[1,64,3584]{2,1,0:T(8,128)(2,1)S(1)}, bf16[1,64,3584]{2,1,0:T(8,128)(2,1)S(1)}, u32[]{:S(2)}, u32[]{:S(2)}) %collective-permute-start.8) | collective-permute-done | bytes 458784 | tf_op jit(solution)/shard_map/ppermute | solution.py:11
  114.5 0.1 bitcast_convert_fusion
  114.5 0.4 convolution_convert_fusion.1
  114.9 0.2 pad_maximum_fusion.1
  115.1 274.2 %all-to-all-done = bf16[64,10,3584]{2,1,0:T(8,128)(2,1)} async-done(((bf16[64,10,3584]{2,1,0:T(8,128)(2,1)}), bf16[64,10,3584]{2,1,0:T(8,128)(2,1)}, u32[]{:S(2)}, u32[]{:S(2)}) %all-to-all-start) | async-done | bytes 4587552 | tf_op jit(solution)/shard_map/all_to_all | solution.py:85
  389.3 3.8 broadcast_in_dim.7
  393.2 12.7 %all-to-all-start.1 = ((bf16[64,10,3584]{2,1,0:T(8,128)(2,1)}), bf16[64,10,3584]{2,1,0:T(8,128)(2,1)}, u32[]{:S(2)}, u32[]{:S(2)}) async-start(bf16[64,10,3584]{2,1,0:T(8,128)(2,1)} %bitcast.68), calls=%async_computation.1 | async-start | bytes 14680064 | tf_op jit(solution)/shard_map/all_to_all | solution.py:86
  405.8 0.0 copy-start.2
  405.9 8.0 %reshape.115 = bf16[640,3584]{1,0:T(8,128)(2,1)} reshape(bf16[64,10,3584]{2,1,0:T(8,128)(2,1)} %all-to-all-done) | data formatting | bytes 9175040 | tf_op jit(solution)/shard_map/reshape | solution.py:89
  413.9 3.6 fusion.13
  417.5 306.8 %all-to-all-done.1 = bf16[64,10,3584]{2,1,0:T(8,128)(2,1)} async-done(((bf16[64,10,3584]{2,1,0:T(8,128)(2,1)}), bf16[64,10,3584]{2,1,0:T(8,128)(2,1)}, u32[]{:S(2)}, u32[]{:S(2)}) %all-to-all-start.1) | async-done | bytes 4587552 | tf_op jit(solution)/shard_map/all_to_all | solution.py:86
  724.4 8.0 %reshape.117 = bf16[640,3584]{1,0:T(8,128)(2,1)} reshape(bf16[64,10,3584]{2,1,0:T(8,128)(2,1)} %all-to-all-done.1) | data formatting | bytes 9175040 | tf_op jit(solution)/shard_map/reshape | solution.py:90
  732.4 8.1 %fusion = bf16[1,128,3584]{2,1,0:T(8,128)(2,1)} fusion(bf16[640,3584]{1,0:T(8,128)(2,1)} %reshape.117, bf16[640,3584]{1,0:T(8,128)(2,1)} %reshape.115, bf16[1,3584,128]{2,1,0:T(8,128)(2,1)S(1)} %copy-done, f32[640,128]{1,0:T(8,128)S(1)} %fusion.13), kind=kOutput, calls=%fused_computation.1 | convolution fusion | flops 1175355392 | bytes 11337728 | tf_op jit(solution)/shard_map/dot_general | solution.py:94
  (17 shorter events, 0.1 us)
Async XLA Ops:
  0.0 732.4 %copy-start = (bf16[1,3584,128]{2,1,0:T(8,128)(2,1)S(1)}, bf16[1,3584,128]{2,1,0:T(8,128)(2,1)}, u32[]{:S(2)}) copy-start(bf16[1,3584,128]{2,1,0:T(8,128)(2,1)} %param.21) | copy-start | bytes 2752516
  2.2 9.6 %collective-permute-start = (bf16[1,64,4]{1,2,0:T(4,128)(2,1)S(1)}, bf16[1,64,4]{1,2,0:T(4,128)(2,1)S(1)}, u32[]{:S(2)}, u32[]{:S(2)}) collective-permute-start(bf16[1,64,4]{1,2,0:T(4,128)(2,1)S(1)} %bitcast.71), channel_id=1, source_target_pairs={{0,64},{64,0},{128,192},{192,128},{256,320},{320,256},{384,448},{4... | collective-permute-start | bytes 1544 | tf_op jit(solution)/shard_map/ppermute | solution.py:11
  6.2 10.5 %collective-permute-start.3 = (bf16[1,64,3584]{2,1,0:T(8,128)(2,1)}, bf16[1,64,3584]{2,1,0:T(8,128)(2,1)S(1)}, u32[]{:S(2)}, u32[]{:S(2)}) collective-permute-start(bf16[1,64,3584]{2,1,0:T(8,128)(2,1)} %param.13), channel_id=1, source_target_pairs={{0,64},{64,0},{128,192},{192,128},{256,320},{320,256},{384,448},{4... | collective-permute-start | bytes 1376264 | tf_op jit(solution)/shard_map/ppermute | solution.py:11
  11.8 12.9 %collective-permute-start.1 = (bf16[1,64,4]{1,2,0:T(4,128)(2,1)S(1)}, bf16[1,64,4]{1,2,0:T(4,128)(2,1)S(1)}, u32[]{:S(2)}, u32[]{:S(2)}) collective-permute-start(bf16[1,64,4]{1,2,0:T(4,128)(2,1)S(1)} %collective-permute-done), channel_id=1, source_target_pairs={{0,128},{64,192},{128,0},{192,64},{256,384},{320,448},{384,256},{4... | collective-permute-start | bytes 1544 | tf_op jit(solution)/shard_map/ppermute | solution.py:11
  16.8 15.2 %collective-permute-start.4 = (bf16[1,64,3584]{2,1,0:T(8,128)(2,1)S(1)}, bf16[1,64,3584]{2,1,0:T(8,128)(2,1)S(1)}, u32[]{:S(2)}, u32[]{:S(2)}) collective-permute-start(bf16[1,64,3584]{2,1,0:T(8,128)(2,1)S(1)} %collective-permute-done.3), channel_id=1, source_target_pairs={{0,128},{64,192},{128,0},{192,64},{256,384},{320,448},{384,256},{4... | collective-permute-start | bytes 1376264 | tf_op jit(solution)/shard_map/ppermute | solution.py:11
  24.7 12.9 %collective-permute-start.2 = (bf16[1,64,4]{1,2,0:T(4,128)(2,1)S(1)}, bf16[1,64,4]{1,2,0:T(4,128)(2,1)S(1)}, u32[]{:S(2)}, u32[]{:S(2)}) collective-permute-start(bf16[1,64,4]{1,2,0:T(4,128)(2,1)S(1)} %collective-permute-done.1), channel_id=1, source_target_pairs={{0,256},{64,320},{128,384},{192,448},{256,0},{320,64},{384,128},{4... | collective-permute-start | bytes 1544 | tf_op jit(solution)/shard_map/ppermute | solution.py:11
  31.9 13.5 %collective-permute-start.5 = (bf16[1,64,3584]{2,1,0:T(8,128)(2,1)S(1)}, bf16[1,64,3584]{2,1,0:T(8,128)(2,1)S(1)}, u32[]{:S(2)}, u32[]{:S(2)}) collective-permute-start(bf16[1,64,3584]{2,1,0:T(8,128)(2,1)S(1)} %collective-permute-done.4), channel_id=1, source_target_pairs={{0,256},{64,320},{128,384},{192,448},{256,0},{320,64},{384,128},{4... | collective-permute-start | bytes 1376264 | tf_op jit(solution)/shard_map/ppermute | solution.py:11
  50.0 20.7 %copy-start.3 = (bf16[1,64,3584]{2,1,0:T(8,128)(2,1)S(1)}, bf16[1,64,3584]{2,1,0:T(8,128)(2,1)}, u32[]{:S(2)}) copy-start(bf16[1,64,3584]{2,1,0:T(8,128)(2,1)} %param.14) | copy-start | bytes 1376260
  50.0 38.8 %copy-start.1 = (bf16[1,64,3584]{2,1,0:T(8,128)(2,1)S(1)}, bf16[1,64,3584]{2,1,0:T(8,128)(2,1)}, u32[]{:S(2)}) copy-start(bf16[1,64,3584]{2,1,0:T(8,128)(2,1)} %param.12) | copy-start | bytes 1376260
  50.0 339.3 %all-to-all-start = ((bf16[64,10,3584]{2,1,0:T(8,128)(2,1)}), bf16[64,10,3584]{2,1,0:T(8,128)(2,1)}, u32[]{:S(2)}, u32[]{:S(2)}) async-start(bf16[64,10,3584]{2,1,0:T(8,128)(2,1)} %bitcast.67), calls=%async_computation | async-start | bytes 14680064 | tf_op jit(solution)/shard_map/all_to_all | solution.py:85
  70.7 13.6 %collective-permute-start.6 = (bf16[1,64,3584]{2,1,0:T(8,128)(2,1)S(1)}, bf16[1,64,3584]{2,1,0:T(8,128)(2,1)S(1)}, u32[]{:S(2)}, u32[]{:S(2)}) collective-permute-start(bf16[1,64,3584]{2,1,0:T(8,128)(2,1)S(1)} %copy-done.3), channel_id=1, source_target_pairs={{0,64},{64,0},{128,192},{192,128},{256,320},{320,256},{384,448},{4... | collective-permute-start | bytes 1376264 | tf_op jit(solution)/shard_map/ppermute | solution.py:11
  84.3 14.2 %collective-permute-start.7 = (bf16[1,64,3584]{2,1,0:T(8,128)(2,1)S(1)}, bf16[1,64,3584]{2,1,0:T(8,128)(2,1)S(1)}, u32[]{:S(2)}, u32[]{:S(2)}) collective-permute-start(bf16[1,64,3584]{2,1,0:T(8,128)(2,1)S(1)} %collective-permute-done.6), channel_id=1, source_target_pairs={{0,128},{64,192},{128,0},{192,64},{256,384},{320,448},{384,256},{4... | collective-permute-start | bytes 1376264 | tf_op jit(solution)/shard_map/ppermute | solution.py:11
  98.5 15.9 %collective-permute-start.8 = (bf16[1,64,3584]{2,1,0:T(8,128)(2,1)S(1)}, bf16[1,64,3584]{2,1,0:T(8,128)(2,1)S(1)}, u32[]{:S(2)}, u32[]{:S(2)}) collective-permute-start(bf16[1,64,3584]{2,1,0:T(8,128)(2,1)S(1)} %collective-permute-done.7), channel_id=1, source_target_pairs={{0,256},{64,320},{128,384},{192,448},{256,0},{320,64},{384,128},{4... | collective-permute-start | bytes 1376264 | tf_op jit(solution)/shard_map/ppermute | solution.py:11
  393.2 331.2 %all-to-all-start.1 = ((bf16[64,10,3584]{2,1,0:T(8,128)(2,1)}), bf16[64,10,3584]{2,1,0:T(8,128)(2,1)}, u32[]{:S(2)}, u32[]{:S(2)}) async-start(bf16[64,10,3584]{2,1,0:T(8,128)(2,1)} %bitcast.68), calls=%async_computation.1 | async-start | bytes 14680064 | tf_op jit(solution)/shard_map/all_to_all | solution.py:86
  405.8 8.0 %copy-start.2 = (bf16[1,3584,128]{2,1,0:T(8,128)(2,1)S(1)}, bf16[1,3584,128]{2,1,0:T(8,128)(2,1)}, u32[]{:S(2)}) copy-start(bf16[1,3584,128]{2,1,0:T(8,128)(2,1)} %param.20) | copy-start | bytes 2752516
where the time goes:
time: 748 us; the launch traced here: 741 us
  waiting for transfers between devices  622 us (83%)
  starting transfers between devices  72.7 us (10%)
  local copies, waits for them, and re-layouts  23.8 us (3%)
  matrix products  14.2 us (2%)
    all_to_all x1, waiting for transfers between devices, body(): lax.all_to_all(joined_grads, 'expert', split_axis=0, concat_axis=0, tiled...  307 us
    all_to_all x1, waiting for transfers between devices, body(): lax.all_to_all(joined_rows, 'expert', split_axis=0, concat_axis=0, tiled=...  274 us
    ppermute x9, waiting for transfers between devices, swapped(): lax.ppermute(value, axis, [(i, i ^ 1 << stride) for i in range(lax.axis_s...  41.1 us
    ppermute x9, starting transfers between devices, swapped(): lax.ppermute(value, axis, [(i, i ^ 1 << stride) for i in range(lax.axis_s...  39.3 us
    all_to_all x1, starting transfers between devices, body(): lax.all_to_all(joined_rows, 'expert', split_axis=0, concat_axis=0, tiled=...  20.7 us
  transfers between devices with their start and end apart: 11, of which 7 were waited for; matrix products, arithmetic and copies ran while one was open for 3% of the time, Pallas kernels for 0%

commit v1 on v0

v1 whole, which is shorter than its diff:
```python
import functools

import jax
import jax.numpy as jnp
from jax import lax
from jax.experimental import pallas as pl
from jax.experimental.pallas import tpu as pltpu
from jax.sharding import PartitionSpec as P

MESH = pl.DeviceIdType.MESH
D = 3584
TOK = 64
CAP = 5
PARTS = 4
LANES = D // PARTS
ROWS = 80
HID = 128


def iota(shape, axis):
    return lax.broadcasted_iota(jnp.int32, shape, axis)


def select_tables(routes, scores, core):
    share = 2.5 * scores / jnp.sum(scores, axis=0, keepdims=True)
    row = iota((8, TOK), 0)
    coef = jnp.zeros((8, TOK), jnp.float32)
    for e in range(4):
        mine = jnp.sum(jnp.where(routes == e, share, 0.0), axis=0, keepdims=True)
        coef = coef + jnp.where(row == e, mine, 0.0)
    coef = coef.astype(jnp.bfloat16)
    taken = jnp.where(coef.astype(jnp.float32) > 0, 1.0, 0.0).astype(jnp.bfloat16)
    token, lane = iota((TOK, 128), 0), iota((TOK, 128), 1) % TOK
    upto = jnp.where(token <= lane, 1.0, 0.0).astype(jnp.bfloat16)
    same = jnp.where(token == lane, 1.0, 0.0).astype(jnp.bfloat16)
    place = jnp.dot(taken, upto, preferred_element_type=jnp.float32) - 1.0
    weight = jnp.dot(coef, same, preferred_element_type=jnp.float32)
    r, lane = iota((16, 128), 0), iota((16, 128), 1)
    left = lane < TOK
    first = CAP * core
    main_ok = left == (r % 16 < 8)
    main_slot = (r % 8 - first).astype(jnp.float32)
    rem_ok = left == (r % 4 < 2)
    rem_slot = (8 + r % 2 - first).astype(jnp.float32)
    main, rem = [], []
    for e in range(4):
        where = jnp.broadcast_to(place[e : e + 1], (16, 128))
        much = jnp.broadcast_to(weight[e : e + 1], (16, 128))
        value = jnp.where(much > 0, jnp.where(left, 1.0, much), 0.0)
        main.append(jnp.where(main_ok & (where == main_slot), value, 0.0))
        rem.append(jnp.where(rem_ok & (where == rem_slot), value, 0.0))
    return jnp.concatenate(main, axis=0), jnp.concatenate(rem, axis=0)


def pack(mb, routes_ref, scores_ref, gain, core, raw, data, packed):
    main, rem = select_tables(routes_ref[...], scores_ref[...], core)
    values = raw[mb].astype(jnp.float32)
    scale = lax.rsqrt(jnp.mean(values * values, axis=-1, keepdims=True) + 1e-06)
    data[mb, 0:TOK, :] = (values * scale * gain).astype(jnp.bfloat16)
    part = (iota((64, 128), 0) % 16) // 4
    total = jnp.zeros((64, LANES), jnp.float32)
    for p in range(PARTS):
        lhs = jnp.concatenate([main, jnp.where(part == p, rem, 0.0)], axis=0).astype(jnp.bfloat16)
        rows = jnp.dot(
            lhs, data[mb, :, p * LANES : (p + 1) * LANES], preferred_element_type=jnp.float32
        )
        packed[mb, :, 16 * p : 16 * p + 16, :] = (
            rows[:64].astype(jnp.bfloat16).reshape(4, 16, LANES)
        )
        total = total + rows[64:]
    packed[mb, :, 64:80, :] = total.astype(jnp.bfloat16).reshape(4, 16, LANES)


def kernel(
    fx, fg, rx, rg, f_routes, r_routes, f_scores, r_scores, gain_ref, wg, wu, out_ref,
    buf, raw, data, packed, gathered, weights, spare, grad, gain_in,
    load_sem, local_sem, gain_sem, swap_sem, first_sem, right_sem, left_sem, x_sem, core_sem, recv_sem,
):
    pipe = lax.axis_index("pipe")
    me = lax.axis_index("expert")
    z, x_lo, core = me // 4, (me // 2) % 2, me % 2
    q, i = z // 4, z % 4
    col = x_lo * 2 + core
    xcol = (1 - x_lo) * 2 + core
    half = i // 2

    def at(zz, xx, cc, pp=None):
        return (pipe if pp is None else pp, zz * 4 + xx * 2 + cc)

    far_pipe = pipe * (1 - core) + (7 - pipe) * core
    far_x = x_lo * (1 - core) + (1 - x_lo) * core
    mirror = at(z, 1 - x_lo, core, 7 - pipe)
    core_mate = at(z, x_lo, 1 - core)
    x_mate = at(z, 1 - x_lo, core)
    z_right = at((z + 1) % 16, x_lo, core)
    z_left = at((z + 15) % 16, x_lo, core)

    loads = [
        pltpu.make_async_copy(fx.at[0], raw.at[0], load_sem.at[0]),
        pltpu.make_async_copy(fg.at[0], data.at[0, pl.ds(TOK, TOK)], load_sem.at[1]),
        pltpu.make_async_copy(rx.at[0], raw.at[1], load_sem.at[2]),
        pltpu.make_async_copy(rg.at[0], data.at[1, pl.ds(TOK, TOK)], load_sem.at[3]),
        pltpu.make_async_copy(wg.at[0], weights.at[:, pl.ds(0, HID)], load_sem.at[4]),
        pltpu.make_async_copy(wu.at[0], weights.at[:, pl.ds(HID, HID)], load_sem.at[5]),
    ]
    for load in loads:
        load.start()

    barrier = pltpu.get_barrier_semaphore()

    def greet(device):
        pl.semaphore_signal(barrier, inc=1, device_id=device, device_id_type=MESH)

    greet(core_mate)
    greet(x_mate)
    greet(mirror)

    @pl.when(i > 0)
    def _():
        greet(z_left)

    @pl.when(i < 3)
    def _():
        greet(z_right)

    @pl.when(i == 0)
    def _():
        for k in range(4):
            greet(at(((q + 3) % 4) * 4 + k, far_x, core, far_pipe))
        for k in (2, 3):
            greet(at(((q + 2) % 4) * 4 + k, far_x, core, far_pipe))

    @pl.when(i == 3)
    def _():
        for k in range(4):
            greet(at(((q + 1) % 4) * 4 + k, far_x, core, far_pipe))
        for k in (0, 1):
            greet(at(((q + 2) % 4) * 4 + k, far_x, core, far_pipe))

    loads[0].wait()
    loads[1].wait()
    pack(0, f_routes, f_scores, gain_ref[...], core, raw, data, packed)
    pl.semaphore_wait(barrier, 7 + (i * (3 - i)) // 2)

    def remote(src, dst, send, recv, device):
        return pltpu.make_async_remote_copy(
            src_ref=src, dst_ref=dst, send_sem=send, recv_sem=recv, device_id=device, device_id_type=MESH
        )

    gain_copy = remote(gain_ref, gain_in, gain_sem.at[0], gain_sem.at[1], mirror)
    gain_copy.start()
    swap = remote(packed.at[1 - core], gathered, swap_sem.at[0], swap_sem.at[1], core_mate)

    def forward(slot, c, send, device):
        return remote(buf.at[slot, c], buf.at[slot, c], send, recv_sem.at[slot, c], device)

    def arrived(slot, c):
        forward(slot, c, core_sem.at[slot, 0], core_mate).wait_recv()

    def go_right(slot):
        return forward(slot, col, right_sem.at[slot], z_right)

    def go_left(slot):
        return forward(slot, col, left_sem.at[slot], z_left)

    def go_x(slot):
        return forward(slot, col, x_sem.at[slot], x_mate)

    def go_core(slot, c, which):
        return forward(slot, c, core_sem.at[slot, which], core_mate)

    far_col = far_x * 2 + core

    def first(step, zz, slot):
        return remote(
            packed.at[core, (q + step) % 4], buf.at[slot, far_col], first_sem.at[step],
            recv_sem.at[slot, far_col], at(zz, far_x, core, far_pipe),
        )

    to_right = first(1, ((q + 1) % 4) * 4, 7 - i + 2 * (1 - half))
    to_left = first(3, ((q + 3) % 4) * 4 + 3, 6 + i + 2 * half)
    to_across = first(
        2, ((q + 2) % 4) * 4 + 3 * (1 - half), half * (15 - i) + (1 - half) * (14 + i)
    )
    to_mirror = first(0, z, i)
    keep = pltpu.make_async_copy(packed.at[0, q], buf.at[i, col], local_sem)

    def merge():
        packed[core] = packed[core] + gathered[...]

    def spread_own():
        @pl.when(i < 3)
        def _():
            go_right(i).start()

        @pl.when(i > 0)
        def _():
            go_left(i).start()

        go_x(i).start()
        go_core(i, col, 0).start()

    @pl.when(core == 1)
    def _():
        swap.start()

    @pl.when(core == 0)
    def _():
        swap.wait_recv()
        merge()
        keep.start()
        to_right.start()
        to_left.start()
        to_across.start()
        keep.wait()
        spread_own()

    loads[2].wait()
    loads[3].wait()
    gain_copy.wait_recv()
    pack(1, r_routes, r_scores, gain_in[...], core, raw, data, packed)

    @pl.when(core == 0)
    def _():
        swap.start()

    @pl.when(core == 1)
    def _():
        swap.wait_recv()
        merge()
        to_mirror.start()
        to_right.start()
        to_left.start()
        to_across.start()

    grad[...] = jnp.zeros_like(grad)

    @pl.when(core == 1)
    def _():
        arrived(i, col)
        spread_own()

    def from_left(slot):
        arrived(slot, col)

        @pl.when(i < 3)
        def _():
            go_right(slot).start()

        go_x(slot).start()
        go_core(slot, col, 0).start()

    def from_right(slot):
        arrived(slot, col)

        @pl.when(i > 0)
        def _():
            go_left(slot).start()

        go_x(slot).start()
        go_core(slot, col, 0).start()

    for step in range(1, 4):

        @pl.when(i >= step)
        def _():
            from_left(i - step)

        @pl.when(i + step <= 3)
        def _():
            from_right(i + step)

    def from_x(slot):
        arrived(slot, xcol)
        go_core(slot, xcol, 1).start()

    def compute(phase):
        block = pl.ds(4 * phase, 4)
        for slot in range(4 * phase, 4 * phase + 4):
            arrived(slot, x_lo * 2 + 1 - core)
            arrived(slot, (1 - x_lo) * 2 + 1 - core)
        out_row, in_row = iota((256, 256), 0), iota((256, 256), 1)
        source = ((out_row % 64) // 4) * 16 + (out_row // 64) * 4 + out_row % 4
        turn = jnp.where(in_row == source, 1.0, 0.0).astype(jnp.bfloat16)
        tail = buf[block, :, 64:80, :].reshape(256, LANES)
        spare[...] = jnp.dot(turn, tail, preferred_element_type=jnp.float32).astype(jnp.bfloat16)
        both = jnp.zeros((320, 2 * HID), jnp.float32)
        for p in range(PARTS):
            rows = jnp.concatenate(
                [
                    buf[block, :, 16 * p : 16 * p + 16, :].reshape(256, LANES),
                    spare[64 * p : 64 * p + 64, :],
                ],
                axis=0,
            )
            both = both + jnp.dot(
                rows, weights[p * LANES : (p + 1) * LANES, :], preferred_element_type=jnp.float32
            )
        gate, up = both[:, :HID], both[:, HID:]
        hidden = gate / (1.0 + jnp.exp(-gate)) * up
        row = iota((320, HID), 0)
        moved = jnp.concatenate(
            [pltpu.roll(hidden[:256], 8, 0), pltpu.roll(hidden[256:], 2, 0)], axis=0
        )
        valid = ((row < 256) & (row % 16 >= 8)) | ((row >= 256) & (row % 4 >= 2))
        side = jnp.where(valid, moved, 0.0).T.astype(jnp.bfloat16)
        for p in range(PARTS):
            rows = jnp.concatenate(
                [
                    buf[block, :, 16 * p : 16 * p + 16, :].reshape(256, LANES),
                    spare[64 * p : 64 * p + 64, :],
                ],
                axis=0,
            )
            lanes = slice(p * LANES, (p + 1) * LANES)
            grad[:, lanes] += jnp.dot(side, rows, preferred_element_type=jnp.float32)

    loads[4].wait()
    loads[5].wait()
    for phase in range(1, 4):
        for k, slot in enumerate((4 * phase, 4 * phase + 2, 4 * phase + 1, 4 * phase + 3)):
            (from_left if k % 2 == 0 else from_right)(slot)
            from_x(4 * phase - 4 + k)
        compute(phase - 1)
    for slot in (12, 14, 13, 15):
        from_x(slot)
    compute(3)
    out_ref[0] = grad[...].astype(jnp.bfloat16)

    gain_copy.wait_send()
    swap.wait_send()
    to_right.wait_send()
    to_left.wait_send()
    to_across.wait_send()

    @pl.when(core == 1)
    def _():
        to_mirror.wait_send()

    for slot in range(16):
        go_x(slot).wait_send()
        go_core(slot, col, 0).wait_send()
        go_core(slot, xcol, 1).wait_send()
    for slot in range(4):

        @pl.when((slot <= i) & (i < 3))
        def _():
            go_right(slot).wait_send()

        @pl.when((slot >= i) & (i > 0))
        def _():
            go_left(slot).wait_send()

    @pl.when(i < 3)
    def _():
        for slot in (4, 5, 8, 9, 12, 13):
            go_right(slot).wait_send()

    @pl.when(i > 0)
    def _():
        for slot in (6, 7, 10, 11, 14, 15):
            go_left(slot).wait_send()


def body(fx, fg, rx, rg, f_routes, r_routes, f_scores, r_scores, gain, w_gate, w_up):
    vmem, hbm = pl.BlockSpec(memory_space=pltpu.VMEM), pl.BlockSpec(memory_space=pl.ANY)
    dma = pltpu.SemaphoreType.DMA
    return pl.pallas_call(
        kernel,
        name="routed_grad",
        out_shape=jax.ShapeDtypeStruct((1, HID, D), jnp.bfloat16),
        in_specs=[hbm] * 4 + [vmem] * 5 + [hbm] * 2,
        out_specs=vmem,
        scratch_shapes=[
            pltpu.VMEM((16, 4, ROWS, LANES), jnp.bfloat16),
            pltpu.VMEM((2, TOK, D), jnp.bfloat16),
            pltpu.VMEM((2, 2 * TOK, D), jnp.bfloat16),
            pltpu.VMEM((2, 4, ROWS, LANES), jnp.bfloat16),
            pltpu.VMEM((4, ROWS, LANES), jnp.bfloat16),
            pltpu.VMEM((D, 2 * HID), jnp.bfloat16),
            pltpu.VMEM((256, LANES), jnp.bfloat16),
            pltpu.VMEM((HID, D), jnp.float32),
            pltpu.VMEM((1, D), jnp.float32),
            dma((6,)), dma, dma((2,)), dma((2,)), dma((4,)), dma((16,)), dma((16,)), dma((16,)),
            dma((16, 2)), dma((16, 4)),
        ],
        compiler_params=pltpu.CompilerParams(
            collective_id=0, has_side_effects=True, vmem_limit_bytes=48 << 20
        ),
        cost_estimate=pl.CostEstimate(flops=6 << 30, bytes_accessed=5 << 20, transcendentals=1 << 17),
    )(
        fx, fg, rx, rg, f_routes[0].T, r_routes[0].T, f_scores[0].T, r_scores[0].T, gain, w_gate, w_up
    )


def solution(mesh):
    rows = P("pipe", "expert", None)
    in_specs = (rows,) * 8 + (P("pipe", None),) + (P("pipe", None, "expert"),) * 2
    return jax.shard_map(body, mesh=mesh, in_specs=in_specs, out_specs=rows, check_vma=False)
```

time: 748 us -> 235 us (0.31)
  waiting for transfers between devices: 622 us -> 0 us
  Pallas kernels: 0 us -> 224 us
  starting transfers between devices: 72.7 us -> 0 us
  matrix products: 14.2 us -> 0 us
  local copies, waits for them, and re-layouts: 23.8 us -> 10.8 us
    all_to_all x2 -> x0, waiting for transfers between devices: 581 us -> none  [the longest x1 307 us: body(): lax.all_to_all(joined_grads, 'expert', split_axis=0, concat_axis=0, tiled...]
    pallas_call x0 -> x1, Pallas kernels: none -> 224 us  [body(): pl.pallas_call(kernel, name='routed_grad', out_shape=jax.ShapeDtypeStruct...]
    ppermute x9 -> x0, waiting for transfers between devices: 41.1 us -> none  [swapped(): lax.ppermute(value, axis, [(i, i ^ 1 << stride) for i in range(lax.axis_s...]
    ppermute x9 -> x0, starting transfers between devices: 39.3 us -> none  [swapped(): lax.ppermute(value, axis, [(i, i ^ 1 << stride) for i in range(lax.axis_s...]
    all_to_all x2 -> x0, starting transfers between devices: 33.4 us -> none  [the longest x1 20.7 us: body(): lax.all_to_all(joined_rows, 'expert', split_axis=0, concat_axis=0, tiled=...]
    reshape x2 -> x0, local copies, waits for them, and re-layouts: 16 us -> none  [the longest x1 8.03 us: body(): flat_rows = received.reshape(-1, features)]
    dot_general x6 -> x0, matrix products: 14.2 us -> none  [the longest x1 8.14 us: body(): lax.dot_general(hidden, flat_grads, (((0,), (0,)), ((), ())), preferred_e...]
    unnamed x8 -> x23, local copies, waits for them, and re-layouts: 0.02 us -> 10.8 us
  transfers between devices with their start and end apart: 11 -> 0, of which waited for: 7 -> 0; matrix products, arithmetic and copies ran while one was open for 3% -> 0% of each run, Pallas kernels for 0% -> 0%
where the time goes in v1:
time: 235 us; the launch traced here: 234 us
  Pallas kernels  224 us (95%)
  local copies, waits for them, and re-layouts  10.8 us (5%)
    pallas_call x1, Pallas kernels, body(): pl.pallas_call(kernel, name='routed_grad', out_shape=jax.ShapeDtypeStruct...  224 us
    unnamed x23, local copies, waits for them, and re-layouts  10.8 us

profile of v1, /device:TPU:1, one launch (start us, length us, event | category | flops | bytes accessed | tf_op | source)
XLA Modules:
  0.0 234.5 jit_solution(12535457627042866014)
XLA Ops:
  0.0 0.0 copy-start.7
  0.0 0.7 copy-done.7
  0.7 0.0 copy-start
  0.7 1.2 copy-done
  1.9 0.0 copy-start.1
  1.9 1.2 copy-done.1
  3.0 0.0 copy-start.2
  3.0 1.0 copy-done.2
  4.1 0.0 copy-start.3
  4.1 1.0 copy-done.3
  5.1 0.0 copy-start.4
  5.1 1.0 copy-done.4
  6.1 0.0 copy-start.5
  6.1 1.0 copy-done.5
  7.1 0.0 copy-start.6
  7.1 0.7 copy-done.6
  7.8 0.0 copy-start.8
  7.8 0.7 copy-done.8
  8.5 0.0 copy-start.9
  8.5 0.7 copy-done.9
  9.2 0.0 copy-start.10
  9.2 0.7 copy-done.10
  9.9 223.6 %routed_grad.1 = bf16[1,128,3584]{2,1,0:T(8,128)(2,1)S(1)} custom-call(bf16[1,64,3584]{2,1,0:T(8,128)(2,1)S(1)} %copy-done.2, bf16[1,64,3584]{2,1,0:T(8,128)(2,1)S(1)} %copy-done.3, bf16[1,64,3584]{2,1,0:T(8,128)(2,1)S(1)} %copy-done.4, bf16[1,64,3584]{2,1,0:T(8,128)(2,1)S(1)} %copy-done.5, s32[8,64]{1,0:T(8,128)S(1)} %bitcast.12, s32[8,64]{1,0:T(8,128)S(1)} %bitcast.13, ...), custom_call_target="tpu_custom_call" | custom-call | flops 6442450944 | bytes 5242880 | tf_op jit(solution)/shard_map/routed_grad/pallas_call | solution.py:368
  233.6 0.9 copy.13
Async XLA Ops:
  0.0 0.7 copy-start.7
  0.7 1.2 copy-start
  1.9 1.2 copy-start.1
  3.0 1.0 copy-start.2
  4.1 1.0 copy-start.3
  5.1 1.0 copy-start.4
  6.1 1.0 copy-start.5
  7.1 0.7 copy-start.6
  7.8 0.7 copy-start.8
  8.5 0.7 copy-start.9
  9.2 0.7 copy-start.10

commit v2 on v1

--- a/solution.py
+++ b/solution.py
@@ -52,8 +52,8 @@
     return jnp.concatenate(main, axis=0), jnp.concatenate(rem, axis=0)
 
 
-def pack(mb, routes_ref, scores_ref, gain, core, raw, data, packed):
-    main, rem = select_tables(routes_ref[...], scores_ref[...], core)
+def pack(mb, routes, scores, gain, core, raw, data, packed):
+    main, rem = select_tables(routes, scores, core)
     values = raw[mb].astype(jnp.float32)
     scale = lax.rsqrt(jnp.mean(values * values, axis=-1, keepdims=True) + 1e-06)
     data[mb, 0:TOK, :] = (values * scale * gain).astype(jnp.bfloat16)
@@ -72,8 +72,8 @@
 
 
 def kernel(
-    fx, fg, rx, rg, f_routes, r_routes, f_scores, r_scores, gain_ref, wg, wu, out_ref,
-    buf, raw, data, packed, gathered, weights, spare, grad, gain_in,
+    fx, fg, rx, rg, routes_0, routes_1, scores_0, scores_1, gain_0, wg, wu, out_ref,
+    buf, routes, scores, gain_ref, raw, data, packed, gathered, weights, spare, grad, gain_in,
     load_sem, local_sem, gain_sem, swap_sem, first_sem, right_sem, left_sem, x_sem, core_sem, recv_sem,
 ):
     pipe = lax.axis_index("pipe")
@@ -87,22 +87,28 @@
     def at(zz, xx, cc, pp=None):
         return (pipe if pp is None else pp, zz * 4 + xx * 2 + cc)
 
-    far_pipe = pipe * (1 - core) + (7 - pipe) * core
+    far_pipe = pipe * (1 - core) + (lax.axis_size("pipe") - 1 - pipe) * core
     far_x = x_lo * (1 - core) + (1 - x_lo) * core
-    mirror = at(z, 1 - x_lo, core, 7 - pipe)
+    mirror = at(z, 1 - x_lo, core, lax.axis_size("pipe") - 1 - pipe)
     core_mate = at(z, x_lo, 1 - core)
     x_mate = at(z, 1 - x_lo, core)
     z_right = at((z + 1) % 16, x_lo, core)
     z_left = at((z + 15) % 16, x_lo, core)
 
-    loads = [
-        pltpu.make_async_copy(fx.at[0], raw.at[0], load_sem.at[0]),
-        pltpu.make_async_copy(fg.at[0], data.at[0, pl.ds(TOK, TOK)], load_sem.at[1]),
-        pltpu.make_async_copy(rx.at[0], raw.at[1], load_sem.at[2]),
-        pltpu.make_async_copy(rg.at[0], data.at[1, pl.ds(TOK, TOK)], load_sem.at[3]),
-        pltpu.make_async_copy(wg.at[0], weights.at[:, pl.ds(0, HID)], load_sem.at[4]),
-        pltpu.make_async_copy(wu.at[0], weights.at[:, pl.ds(HID, HID)], load_sem.at[5]),
-    ]
+    sources = (
+        (routes_0, routes.at[0]),
+        (scores_0, scores.at[0]),
+        (fx.at[0], raw.at[0]),
+        (gain_0, gain_ref),
+        (fg.at[0], data.at[0, pl.ds(TOK, TOK)]),
+        (routes_1, routes.at[1]),
+        (scores_1, scores.at[1]),
+        (rx.at[0], raw.at[1]),
+        (rg.at[0], data.at[1, pl.ds(TOK, TOK)]),
+        (wg.at[0], weights.at[:, pl.ds(0, HID)]),
+        (wu.at[0], weights.at[:, pl.ds(HID, HID)]),
+    )
+    loads = [pltpu.make_async_copy(a, b, load_sem.at[k]) for k, (a, b) in enumerate(sources)]
     for load in loads:
         load.start()
 
@@ -137,9 +143,9 @@
         for k in (0, 1):
             greet(at(((q + 2) % 4) * 4 + k, far_x, core, far_pipe))
 
-    loads[0].wait()
-    loads[1].wait()
-    pack(0, f_routes, f_scores, gain_ref[...], core, raw, data, packed)
+    for load in loads[:5]:
+        load.wait()
+    pack(0, routes[0], scores[0], gain_ref[...], core, raw, data, packed)
     pl.semaphore_wait(barrier, 7 + (i * (3 - i)) // 2)
 
     def remote(src, dst, send, recv, device):
@@ -177,13 +183,14 @@
             recv_sem.at[slot, far_col], at(zz, far_x, core, far_pipe),
         )
 
-    to_right = first(1, ((q + 1) % 4) * 4, 7 - i + 2 * (1 - half))
-    to_left = first(3, ((q + 3) % 4) * 4 + 3, 6 + i + 2 * half)
+    own = 9 - i
+    to_right = first(1, ((q + 1) % 4) * 4, 13 - i)
+    to_left = first(3, ((q + 3) % 4) * 4 + 3, 5 - i)
     to_across = first(
-        2, ((q + 2) % 4) * 4 + 3 * (1 - half), half * (15 - i) + (1 - half) * (14 + i)
+        2, ((q + 2) % 4) * 4 + 3 * (1 - half), half * (17 - i) + (1 - half) * (1 - i)
     )
-    to_mirror = first(0, z, i)
-    keep = pltpu.make_async_copy(packed.at[0, q], buf.at[i, col], local_sem)
+    to_mirror = first(0, z, own)
+    keep = pltpu.make_async_copy(packed.at[0, q], buf.at[own, col], local_sem)
 
     def merge():
         packed[core] = packed[core] + gathered[...]
@@ -191,14 +198,14 @@
     def spread_own():
         @pl.when(i < 3)
         def _():
-            go_right(i).start()
+            go_right(own).start()
 
         @pl.when(i > 0)
         def _():
-            go_left(i).start()
-
-        go_x(i).start()
-        go_core(i, col, 0).start()
+            go_left(own).start()
+
+        go_x(own).start()
+        go_core(own, col, 0).start()
 
     @pl.when(core == 1)
     def _():
@@ -211,14 +218,14 @@
         keep.start()
         to_right.start()
         to_left.start()
-        to_across.start()
         keep.wait()
         spread_own()
-
-    loads[2].wait()
-    loads[3].wait()
+        to_across.start()
+
+    for load in loads[5:9]:
+        load.wait()
     gain_copy.wait_recv()
-    pack(1, r_routes, r_scores, gain_in[...], core, raw, data, packed)
+    pack(1, routes[1], scores[1], gain_in[...], core, raw, data, packed)
 
     @pl.when(core == 0)
     def _():
@@ -237,7 +244,7 @@
 
     @pl.when(core == 1)
     def _():
-        arrived(i, col)
+        arrived(own, col)
         spread_own()
 
     def from_left(slot):
@@ -259,16 +266,6 @@
 
         go_x(slot).start()
         go_core(slot, col, 0).start()
-
-    for step in range(1, 4):
-
-        @pl.when(i >= step)
-        def _():
-            from_left(i - step)
-
-        @pl.when(i + step <= 3)
-        def _():
-            from_right(i + step)
 
     def from_x(slot):
         arrived(slot, xcol)
@@ -276,9 +273,9 @@
 
     def compute(phase):
         block = pl.ds(4 * phase, 4)
-        for slot in range(4 * phase, 4 * phase + 4):
-            arrived(slot, x_lo * 2 + 1 - core)
-            arrived(slot, (1 - x_lo) * 2 + 1 - core)
+        for k in range(4):
+            arrived(4 * phase + k, x_lo * 2 + 1 - core)
+            arrived(4 * phase + k, (1 - x_lo) * 2 + 1 - core)
         out_row, in_row = iota((256, 256), 0), iota((256, 256), 1)
         source = ((out_row % 64) // 4) * 16 + (out_row // 64) * 4 + out_row % 4
         turn = jnp.where(in_row == source, 1.0, 0.0).astype(jnp.bfloat16)
@@ -315,16 +312,40 @@
             lanes = slice(p * LANES, (p + 1) * LANES)
             grad[:, lanes] += jnp.dot(side, rows, preferred_element_type=jnp.float32)
 
-    loads[4].wait()
-    loads[5].wait()
-    for phase in range(1, 4):
-        for k, slot in enumerate((4 * phase, 4 * phase + 2, 4 * phase + 1, 4 * phase + 3)):
-            (from_left if k % 2 == 0 else from_right)(slot)
-            from_x(4 * phase - 4 + k)
-        compute(phase - 1)
-    for slot in (12, 14, 13, 15):
-        from_x(slot)
-    compute(3)
+    for load in loads[9:]:
+        load.wait()
+    def along_x(step):
+        if step < 0:
+            from_x(own)
+            return
+
+        @pl.when(step <= 5 + i)
+        def _():
+            from_x(own + 1 + step)
+
+        @pl.when(step <= 8 - i)
+        def _():
+            from_x(own - 1 - step)
+
+    for step in range(9):
+
+        @pl.when(step <= 5 + i)
+        def _():
+            from_left(own + 1 + step)
+
+        @pl.when(step <= 8 - i)
+        def _():
+            from_right(own - 1 - step)
+
+        along_x(step - 1)
+        if step == 4:
+            compute(2 - half)
+        if step == 6:
+            compute(1 + half)
+        if step == 8:
+            compute(3 - 3 * half)
+    along_x(8)
+    compute(3 * half)
     out_ref[0] = grad[...].astype(jnp.bfloat16)
 
     gain_copy.wait_send()
@@ -341,24 +362,14 @@
         go_x(slot).wait_send()
         go_core(slot, col, 0).wait_send()
         go_core(slot, xcol, 1).wait_send()
-    for slot in range(4):
-
-        @pl.when((slot <= i) & (i < 3))
+    for slot in range(16):
+
+        @pl.when((slot >= own) & (i < 3))
         def _():
             go_right(slot).wait_send()
 
-        @pl.when((slot >= i) & (i > 0))
-        def _():
-            go_left(slot).wait_send()
-
-    @pl.when(i < 3)
-    def _():
-        for slot in (4, 5, 8, 9, 12, 13):
-            go_right(slot).wait_send()
-
-    @pl.when(i > 0)
-    def _():
-        for slot in (6, 7, 10, 11, 14, 15):
+        @pl.when((slot <= own) & (i > 0))
+        def _():
             go_left(slot).wait_send()
 
 
@@ -369,10 +380,13 @@
         kernel,
         name="routed_grad",
         out_shape=jax.ShapeDtypeStruct((1, HID, D), jnp.bfloat16),
-        in_specs=[hbm] * 4 + [vmem] * 5 + [hbm] * 2,
+        in_specs=[hbm] * 11,
         out_specs=vmem,
         scratch_shapes=[
             pltpu.VMEM((16, 4, ROWS, LANES), jnp.bfloat16),
+            pltpu.VMEM((2, 8, TOK), jnp.int32),
+            pltpu.VMEM((2, 8, TOK), jnp.float32),
+            pltpu.VMEM((1, D), jnp.float32),
             pltpu.VMEM((2, TOK, D), jnp.bfloat16),
             pltpu.VMEM((2, 2 * TOK, D), jnp.bfloat16),
             pltpu.VMEM((2, 4, ROWS, LANES), jnp.bfloat16),
@@ -381,11 +395,11 @@
             pltpu.VMEM((256, LANES), jnp.bfloat16),
             pltpu.VMEM((HID, D), jnp.float32),
             pltpu.VMEM((1, D), jnp.float32),
-            dma((6,)), dma, dma((2,)), dma((2,)), dma((4,)), dma((16,)), dma((16,)), dma((16,)),
+            dma((11,)), dma, dma((2,)), dma((2,)), dma((4,)), dma((16,)), dma((16,)), dma((16,)),
             dma((16, 2)), dma((16, 4)),
         ],
         compiler_params=pltpu.CompilerParams(
-            collective_id=0, has_side_effects=True, vmem_limit_bytes=48 << 20
+            collective_id=0, has_side_effects=True, vmem_limit_bytes=63 << 20
         ),
         cost_estimate=pl.CostEstimate(flops=6 << 30, bytes_accessed=5 << 20, transcendentals=1 << 17),
     )(

time: 235 us -> 102 us (0.43)
  Pallas kernels: 224 us -> 100 us
  local copies, waits for them, and re-layouts: 10.8 us -> 2.16 us
    pallas_call x1, Pallas kernels: 224 us -> 100 us  [body(): pl.pallas_call(kernel, name='routed_grad', out_shape=jax.ShapeDtypeStruct...]
    unnamed x23 -> x1, local copies, waits for them, and re-layouts: 10.8 us -> 2.16 us
where the time goes in v2:
time: 102 us
  Pallas kernels  100 us (98%)
  local copies, waits for them, and re-layouts  2.16 us (2%)
    pallas_call x1, Pallas kernels, body(): pl.pallas_call(kernel, name='routed_grad', out_shape=jax.ShapeDtypeStruct...  100 us
    unnamed x1, local copies, waits for them, and re-layouts  2.16 us

profile of v2, /device:TPU:1, one launch (start us, length us, event | category | flops | bytes accessed | tf_op | source)
XLA Modules:
  0.0 102.2 jit_solution(16371384490306629784)
XLA Ops:
  0.0 100.1 %routed_grad.1 = bf16[1,128,3584]{2,1,0:T(8,128)(2,1)} custom-call(bf16[1,64,3584]{2,1,0:T(8,128)(2,1)} %fx.1, bf16[1,64,3584]{2,1,0:T(8,128)(2,1)} %fg.1, bf16[1,64,3584]{2,1,0:T(8,128)(2,1)} %rx.1, bf16[1,64,3584]{2,1,0:T(8,128)(2,1)} %rg.1, s32[8,64]{1,0:T(8,128)} %bitcast.12, s32[8,64]{1,0:T(8,128)} %bitcast.13, f32[8,64]{1,0:T(8,128)} %bitcast.14, ...), custom_call_target="tpu_custom_call" | custom-call | flops 6442450944 | bytes 5242880 | tf_op jit(solution)/shard_map/routed_grad/pallas_call | solution.py:379
  100.1 2.2 %copy.13 = bf16[1,128,3584]{2,1,0:T(8,128)(2,1)} copy(bf16[1,128,3584]{2,1,0:T(8,128)(2,1)} %routed_grad.1) | data formatting | bytes 1835008

commit v3 on v2

v3 whole, which is shorter than its diff:
```python
import functools

import jax
import jax.numpy as jnp
from jax import lax
from jax.experimental import pallas as pl
from jax.experimental.pallas import tpu as pltpu
from jax.sharding import PartitionSpec as P

MESH = pl.DeviceIdType.MESH
AHEAD = 1
D = 3584
TOK = 64
CAP = 5
PARTS = 4
LANES = D // PARTS
ROWS = 80
HID = 128


def iota(shape, axis):
    return lax.broadcasted_iota(jnp.int32, shape, axis)


def select_tables(routes_ref, scores_ref):
    place = jnp.zeros((8, 4 * TOK), jnp.float32)
    weight = jnp.zeros((8, 4 * TOK), jnp.float32)
    row = iota((8, TOK), 0)
    token, lane = iota((TOK, 4 * TOK), 0), iota((TOK, 4 * TOK), 1)
    for h in range(2):
        routes, scores = routes_ref[h], scores_ref[h]
        share = 2.5 * scores / jnp.sum(scores, axis=0, keepdims=True)
        coef = jnp.zeros((8, TOK), jnp.float32)
        for e in range(4):
            mine = jnp.sum(jnp.where(routes == e, share, 0.0), axis=0, keepdims=True)
            coef = coef + jnp.where(row == e, mine, 0.0)
        coef = coef.astype(jnp.bfloat16)
        taken = jnp.where(coef.astype(jnp.float32) > 0, 1.0, 0.0).astype(jnp.bfloat16)
        here = (lane // TOK) % 2 == h
        upto = jnp.where(here & (token <= lane % TOK), 1.0, 0.0).astype(jnp.bfloat16)
        same = jnp.where(here & (token == lane % TOK), 1.0, 0.0).astype(jnp.bfloat16)
        place = place + jnp.dot(taken, upto, preferred_element_type=jnp.float32)
        weight = weight + jnp.dot(coef, same, preferred_element_type=jnp.float32)
    lane = iota((8, 4 * TOK), 1)
    place = place + jnp.where((lane // TOK) % 2 == 1, CAP - 1.0, -1.0)
    r, lane = iota((16, 4 * TOK), 0), iota((16, 4 * TOK), 1)
    left = lane < 2 * TOK
    main_ok = left == (r < 8)
    main_slot = (r % 8).astype(jnp.float32)
    rem_ok = left == (r % 4 < 2)
    rem_slot = (8 + r % 2).astype(jnp.float32)
    main, rem = [], []
    for e in range(4):
        where = jnp.broadcast_to(place[e : e + 1], (16, 4 * TOK))
        much = jnp.broadcast_to(weight[e : e + 1], (16, 4 * TOK))
        value = jnp.where(much > 0, jnp.where(left, 1.0, much), 0.0)
        main.append(jnp.where(main_ok & (where == main_slot), value, 0.0))
        rem.append(jnp.where(rem_ok & (where == rem_slot), value, 0.0))
    return jnp.concatenate(main, axis=0), jnp.concatenate(rem, axis=0)


def pack(main, rem, data, packed):
    part = (iota((64, 4 * TOK), 0) % 16) // 4
    total = jnp.zeros((64, LANES), jnp.float32)
    for p in range(PARTS):
        lhs = jnp.concatenate([main, jnp.where(part == p, rem, 0.0)], axis=0).astype(jnp.bfloat16)
        rows = jnp.dot(
            lhs, data[:, p * LANES : (p + 1) * LANES], preferred_element_type=jnp.float32
        )
        packed[:, 16 * p : 16 * p + 16, :] = rows[:64].astype(jnp.bfloat16).reshape(4, 16, LANES)
        total = total + rows[64:]
    packed[:, 64:80, :] = total.astype(jnp.bfloat16).reshape(4, 16, LANES)


def kernel(
    fx, fg, rx, rg, routes_0, routes_1, scores_0, scores_1, gain_0, wg, wu, out_ref,
    buf, routes, scores, gain, gain_in, raw, data, packed, weights, spare, grad,
    load_sem, local_sem, gain_sem, swap_send, swap_recv, first_sem, right_sem, left_sem, x_sem, core_sem, recv_sem,
):
    pipe = lax.axis_index("pipe")
    me = lax.axis_index("expert")
    z, x_lo, core = me // 4, (me // 2) % 2, me % 2
    q, i = z // 4, z % 4
    col = x_lo * 2 + core
    xcol = (1 - x_lo) * 2 + core
    half = i // 2

    def at(zz, xx, cc, pp=None):
        return (pipe if pp is None else pp, zz * 4 + xx * 2 + cc)

    far_pipe = pipe * (1 - core) + (lax.axis_size("pipe") - 1 - pipe) * core
    far_x = x_lo * (1 - core) + (1 - x_lo) * core
    mirror = at(z, 1 - x_lo, core, lax.axis_size("pipe") - 1 - pipe)
    core_mate = at(z, x_lo, 1 - core)
    x_mate = at(z, 1 - x_lo, core)
    z_right = at((z + 1) % 16, x_lo, core)
    z_left = at((z + 15) % 16, x_lo, core)

    def load(k, source, target):
        return pltpu.make_async_copy(source, target, load_sem.at[k])

    tokens = pl.ds(pl.multiple_of(core * TOK, TOK), TOK)
    mine_to = (routes.at[core], scores.at[core], raw.at[tokens], data.at[1, tokens])
    micro = ((routes_0, scores_0, fx.at[0], fg.at[0]), (routes_1, scores_1, rx.at[0], rg.at[0]))
    load_gain = load(4, gain_0, gain)
    load_gate = load(5, wg.at[0], weights.at[:, pl.ds(0, HID)])
    load_up = load(6, wu.at[0], weights.at[:, pl.ds(HID, HID)])
    for h in range(2):

        @pl.when(core == h)
        def _():
            for k in range(4):
                load(k, micro[h][k], mine_to[k]).start()

    load_gain.start()

    barrier = pltpu.get_barrier_semaphore()

    def greet(device):
        pl.semaphore_signal(barrier, inc=1, device_id=device, device_id_type=MESH)

    greet(core_mate)
    greet(x_mate)
    greet(mirror)

    @pl.when(i > 0)
    def _():
        greet(z_left)

    @pl.when(i < 3)
    def _():
        greet(z_right)

    @pl.when(i == 0)
    def _():
        for k in range(4):
            greet(at(((q + 3) % 4) * 4 + k, far_x, core, far_pipe))
        for k in (2, 3):
            greet(at(((q + 2) % 4) * 4 + k, far_x, core, far_pipe))

    @pl.when(i == 3)
    def _():
        for k in range(4):
            greet(at(((q + 1) % 4) * 4 + k, far_x, core, far_pipe))
        for k in (0, 1):
            greet(at(((q + 2) % 4) * 4 + k, far_x, core, far_pipe))

    pl.semaphore_wait(barrier, 7 + (i * (3 - i)) // 2)

    def remote(src, dst, send, recv, device):
        return pltpu.make_async_remote_copy(
            src_ref=src, dst_ref=dst, send_sem=send, recv_sem=recv, device_id=device, device_id_type=MESH
        )

    def swap(k, h):
        return remote(micro[1 - h][k], mine_to[k], swap_send.at[k], swap_recv.at[k], core_mate)

    for h in range(2):

        @pl.when(core == h)
        def _():
            for k in range(4):
                swap(k, h).start()

    load_gain.wait()
    gain_copy = remote(gain, gain_in, gain_sem.at[0], gain_sem.at[1], mirror)
    gain_copy.start()
    load_gate.start()
    load_up.start()

    def forward(slot, c, send, device):
        return remote(buf.at[slot, c], buf.at[slot, c], send, recv_sem.at[slot, c], device)

    def arrived(slot, c):
        forward(slot, c, core_sem.at[slot, 0], core_mate).wait_recv()

    def go_right(slot):
        return forward(slot, col, right_sem.at[slot], z_right)

    def go_left(slot):
        return forward(slot, col, left_sem.at[slot], z_left)

    def go_x(slot):
        return forward(slot, col, x_sem.at[slot], x_mate)

    def go_core(slot, c, which):
        return forward(slot, c, core_sem.at[slot, which], core_mate)

    far_col = far_x * 2 + core

    def first(step, zz, slot):
        return remote(
            packed.at[(q + step) % 4], buf.at[slot, far_col], first_sem.at[step],
            recv_sem.at[slot, far_col], at(zz, far_x, core, far_pipe),
        )

    own = 9 - i
    to_right = first(1, ((q + 1) % 4) * 4, 13 - i)
    to_left = first(3, ((q + 3) % 4) * 4 + 3, 5 - i)
    to_across = first(
        2, ((q + 2) % 4) * 4 + 3 * (1 - half), half * (17 - i) + (1 - half) * (1 - i)
    )
    to_mirror = first(0, z, own)
    keep = pltpu.make_async_copy(packed.at[q], buf.at[own, col], local_sem)

    def spread_own():
        @pl.when(i < 3)
        def _():
            go_right(own).start()

        @pl.when(i > 0)
        def _():
            go_left(own).start()

        go_x(own).start()
        go_core(own, col, 0).start()

    def here(k):
        load(k, micro[0][k], mine_to[k]).wait()
        swap(k, 0).wait_recv()

    here(0)
    here(1)
    main, rem = select_tables(routes, scores)
    here(2)
    values = raw[...].astype(jnp.float32)
    scale = lax.rsqrt(jnp.mean(values * values, axis=-1, keepdims=True) + 1e-06)
    gain_copy.wait_recv()
    factor = jnp.where(core == 0, gain[...], gain_in[...])
    data[0] = (values * scale * factor).astype(jnp.bfloat16)
    here(3)
    pack(main, rem, data.reshape(4 * TOK, D), packed)
    @pl.when(core == 0)
    def _():
        keep.start()
        keep.wait()
        spread_own()

    @pl.when(core == 1)
    def _():
        to_mirror.start()

    def issue(point):
        for copy, k in ((to_right, 3 - i), (to_left, i), (to_across, 4 + half * (3 - i) + (1 - half) * i)):
            due = (k <= AHEAD) if point == 0 else (k == AHEAD + point)

            @pl.when(due)
            def _():
                copy.start()

    issue(0)
    grad[...] = jnp.zeros_like(grad)

    @pl.when(core == 1)
    def _():
        arrived(own, col)
        spread_own()

    def from_left(slot):
        arrived(slot, col)

        @pl.when(i < 3)
        def _():
            go_right(slot).start()

        go_x(slot).start()
        go_core(slot, col, 0).start()

    def from_right(slot):
        arrived(slot, col)

        @pl.when(i > 0)
        def _():
            go_left(slot).start()

        go_x(slot).start()
        go_core(slot, col, 0).start()

    def from_x(slot):
        arrived(slot, xcol)
        go_core(slot, xcol, 1).start()

    def compute(base, slots, last=False):
        block = pl.ds(base, slots)
        main, rest = slots * 64, slots * 16
        for k in range(slots):
            arrived(base + k, x_lo * 2 + 1 - core)
            arrived(base + k, (1 - x_lo) * 2 + 1 - core)
        out_row, in_row = iota((main, main), 0), iota((main, main), 1)
        source = ((out_row % rest) // 4) * 16 + (out_row // rest) * 4 + out_row % 4
        turn = jnp.where(in_row == source, 1.0, 0.0).astype(jnp.bfloat16)
        tail = buf[block, :, 64:80, :].reshape(main, LANES)
        spare[:main, :] = jnp.dot(turn, tail, preferred_element_type=jnp.float32).astype(jnp.bfloat16)

        def rows_of(p):
            return jnp.concatenate(
                [
                    buf[block, :, 16 * p : 16 * p + 16, :].reshape(main, LANES),
                    spare[rest * p : rest * p + rest, :],
                ],
                axis=0,
            )

        both = jnp.zeros((main + rest, 2 * HID), jnp.float32)
        for p in range(PARTS):
            both = both + jnp.dot(
                rows_of(p), weights[p * LANES : (p + 1) * LANES, :], preferred_element_type=jnp.float32
            )
        gate, up = both[:, :HID], both[:, HID:]
        hidden = gate / (1.0 + jnp.exp(-gate)) * up
        row = iota((main + rest, HID), 0)
        moved = jnp.concatenate(
            [pltpu.roll(hidden[:main], 8, 0), pltpu.roll(hidden[main:], 2, 0)], axis=0
        )
        valid = ((row < main) & (row % 16 >= 8)) | ((row >= main) & (row % 4 >= 2))
        side = jnp.where(valid, moved, 0.0).T.astype(jnp.bfloat16)
        for p in range(PARTS):
            lanes = slice(p * LANES, (p + 1) * LANES)
            total = grad[:, lanes] + jnp.dot(side, rows_of(p), preferred_element_type=jnp.float32)
            if last:
                out_ref[0, :, lanes] = total.astype(jnp.bfloat16)
            else:
                grad[:, lanes] = total

    load_gate.wait()
    load_up.wait()
    def along_x(step):
        if step < 0:
            from_x(own)
            return

        @pl.when(step <= 5 + i)
        def _():
            from_x(own + 1 + step)

        @pl.when(step <= 8 - i)
        def _():
            from_x(own - 1 - step)

    for step in range(9):

        @pl.when(step <= 5 + i)
        def _():
            from_left(own + 1 + step)

        @pl.when(step <= 8 - i)
        def _():
            from_right(own - 1 - step)

        issue(step + 1)
        along_x(step - 1)
        if step == 4:
            compute(8 - 4 * half, 4)
        if step == 6:
            compute(4 + 4 * half, 4)
        if step == 7:
            compute(12 - 12 * half, 4)
        if step == 8:
            compute(2 + 10 * half, 2)
    along_x(8)
    compute(14 * half, 2, last=True)

    gain_copy.wait_send()
    for k in range(4):
        swap(k, 0).wait_send()
    to_right.wait_send()
    to_left.wait_send()
    to_across.wait_send()

    @pl.when(core == 1)
    def _():
        to_mirror.wait_send()

    for slot in range(16):
        go_x(slot).wait_send()
        go_core(slot, col, 0).wait_send()
        go_core(slot, xcol, 1).wait_send()
    for slot in range(16):

        @pl.when((slot >= own) & (i < 3))
        def _():
            go_right(slot).wait_send()

        @pl.when((slot <= own) & (i > 0))
        def _():
            go_left(slot).wait_send()


def body(fx, fg, rx, rg, f_routes, r_routes, f_scores, r_scores, gain, w_gate, w_up):
    vmem, hbm = pl.BlockSpec(memory_space=pltpu.VMEM), pl.BlockSpec(memory_space=pl.ANY)
    dma = pltpu.SemaphoreType.DMA
    return pl.pallas_call(
        kernel,
        name="routed_grad",
        out_shape=jax.ShapeDtypeStruct((1, HID, D), jnp.bfloat16),
        in_specs=[hbm] * 11,
        out_specs=vmem,
        scratch_shapes=[
            pltpu.VMEM((16, 4, ROWS, LANES), jnp.bfloat16),
            pltpu.VMEM((2, 8, TOK), jnp.int32),
            pltpu.VMEM((2, 8, TOK), jnp.float32),
            pltpu.VMEM((1, D), jnp.float32),
            pltpu.VMEM((1, D), jnp.float32),
            pltpu.VMEM((2 * TOK, D), jnp.bfloat16),
            pltpu.VMEM((2, 2 * TOK, D), jnp.bfloat16),
            pltpu.VMEM((4, ROWS, LANES), jnp.bfloat16),
            pltpu.VMEM((D, 2 * HID), jnp.bfloat16),
            pltpu.VMEM((256, LANES), jnp.bfloat16),
            pltpu.VMEM((HID, D), jnp.float32),
            dma((7,)), dma, dma((2,)), dma((4,)), dma((4,)), dma((4,)), dma((16,)), dma((16,)), dma((16,)),
            dma((16, 2)), dma((16, 4)),
        ],
        compiler_params=pltpu.CompilerParams(
            collective_id=0, has_side_effects=True, vmem_limit_bytes=63 << 20
        ),
        cost_estimate=pl.CostEstimate(flops=6 << 30, bytes_accessed=5 << 20, transcendentals=1 << 17),
    )(
        fx, fg, rx, rg, f_routes[0].T, r_routes[0].T, f_scores[0].T, r_scores[0].T, gain, w_gate, w_up
    )


def solution(mesh):
    rows = P("pipe", "expert", None)
    in_specs = (rows,) * 8 + (P("pipe", None),) + (P("pipe", None, "expert"),) * 2
    return jax.shard_map(body, mesh=mesh, in_specs=in_specs, out_specs=rows, check_vma=False)
```

time: 102 us -> 89 us (0.87); the launches traced: 102 us -> 87.8 us
  Pallas kernels: 100 us -> 85.7 us
    pallas_call x1, Pallas kernels: 100 us -> 85.7 us  [body(): pl.pallas_call(kernel, name='routed_grad', out_shape=jax.ShapeDtypeStruct...]
where the time goes in v3:
time: 89 us; the launch traced here: 87.8 us
  Pallas kernels  85.7 us (96%)
  local copies, waits for them, and re-layouts  2.16 us (2%)
    pallas_call x1, Pallas kernels, body(): pl.pallas_call(kernel, name='routed_grad', out_shape=jax.ShapeDtypeStruct...  85.7 us
    unnamed x1, local copies, waits for them, and re-layouts  2.16 us

profile of v3, /device:TPU:1, one launch (start us, length us, event | category | flops | bytes accessed | tf_op | source)
XLA Modules:
  0.0 87.8 jit_solution(322218602682389980)
XLA Ops:
  0.0 85.7 %routed_grad.1 = bf16[1,128,3584]{2,1,0:T(8,128)(2,1)} custom-call(bf16[1,64,3584]{2,1,0:T(8,128)(2,1)} %fx.1, bf16[1,64,3584]{2,1,0:T(8,128)(2,1)} %fg.1, bf16[1,64,3584]{2,1,0:T(8,128)(2,1)} %rx.1, bf16[1,64,3584]{2,1,0:T(8,128)(2,1)} %rg.1, s32[8,64]{1,0:T(8,128)} %bitcast.12, s32[8,64]{1,0:T(8,128)} %bitcast.13, f32[8,64]{1,0:T(8,128)} %bitcast.14, ...), custom_call_target="tpu_custom_call" | custom-call | flops 6442450944 | bytes 5242880 | tf_op jit(solution)/shard_map/routed_grad/pallas_call | solution.py:392
  85.7 2.2 %copy.13 = bf16[1,128,3584]{2,1,0:T(8,128)(2,1)} copy(bf16[1,128,3584]{2,1,0:T(8,128)(2,1)} %routed_grad.1) | data formatting | bytes 1835008

commit v4 on v3

--- a/solution.py
+++ b/solution.py
@@ -15,6 +15,7 @@
 PARTS = 4
 LANES = D // PARTS
 ROWS = 80
+PIECES = ((0, 48), (48, 32))
 HID = 128
 
 
@@ -74,7 +75,7 @@
 
 def kernel(
     fx, fg, rx, rg, routes_0, routes_1, scores_0, scores_1, gain_0, wg, wu, out_ref,
-    buf, routes, scores, gain, gain_in, raw, data, packed, weights, spare, grad,
+    buf, routes, scores, gain, gain_out, gain_in, raw, data, packed, weights, spare, grad,
     load_sem, local_sem, gain_sem, swap_send, swap_recv, first_sem, right_sem, left_sem, x_sem, core_sem, recv_sem,
 ):
     pipe = lax.axis_index("pipe")
@@ -163,36 +164,48 @@
                 swap(k, h).start()
 
     load_gain.wait()
-    gain_copy = remote(gain, gain_in, gain_sem.at[0], gain_sem.at[1], mirror)
+    gain_out[...] = gain[...]
+    gain_copy = remote(gain_out, gain_in, gain_sem.at[0], gain_sem.at[1], mirror)
     gain_copy.start()
     load_gate.start()
     load_up.start()
 
-    def forward(slot, c, send, device):
-        return remote(buf.at[slot, c], buf.at[slot, c], send, recv_sem.at[slot, c], device)
-
-    def arrived(slot, c):
-        forward(slot, c, core_sem.at[slot, 0], core_mate).wait_recv()
-
-    def go_right(slot):
-        return forward(slot, col, right_sem.at[slot], z_right)
-
-    def go_left(slot):
-        return forward(slot, col, left_sem.at[slot], z_left)
-
-    def go_x(slot):
-        return forward(slot, col, x_sem.at[slot], x_mate)
+    def piece(slot, c, h):
+        return buf.at[slot, c, pl.ds(*PIECES[h])]
+
+    def forward(slot, c, h, send, device):
+        here = piece(slot, c, h)
+        return remote(here, here, send, recv_sem.at[slot, c, h], device)
+
+    def arrived(slot, c, h):
+        forward(slot, c, h, core_sem.at[slot, 0], core_mate).wait_recv()
+
+    def go_right(slot, h):
+        return forward(slot, col, h, right_sem.at[slot, h], z_right)
+
+    def go_left(slot, h):
+        return forward(slot, col, h, left_sem.at[slot, h], z_left)
+
+    def go_x(slot, h):
+        return forward(slot, col, h, x_sem.at[slot, h], x_mate)
 
     def go_core(slot, c, which):
-        return forward(slot, c, core_sem.at[slot, which], core_mate)
+        whole = buf.at[slot, c]
+        return remote(whole, whole, core_sem.at[slot, which], recv_sem.at[slot, c, 0], core_mate)
+
+    def from_core(slot, c):
+        go_core(slot, c, 0).wait_recv()
 
     far_col = far_x * 2 + core
 
     def first(step, zz, slot):
-        return remote(
-            packed.at[(q + step) % 4], buf.at[slot, far_col], first_sem.at[step],
-            recv_sem.at[slot, far_col], at(zz, far_x, core, far_pipe),
-        )
+        return [
+            remote(
+                packed.at[(q + step) % 4, pl.ds(*PIECES[h])], buf.at[slot, far_col, pl.ds(*PIECES[h])],
+                first_sem.at[step, h], recv_sem.at[slot, far_col, h], at(zz, far_x, core, far_pipe),
+            )
+            for h in range(2)
+        ]
 
     own = 9 - i
     to_right = first(1, ((q + 1) % 4) * 4, 13 - i)
@@ -203,17 +216,18 @@
     to_mirror = first(0, z, own)
     keep = pltpu.make_async_copy(packed.at[q], buf.at[own, col], local_sem)
 
-    def spread_own():
+    def spread_own(h):
         @pl.when(i < 3)
         def _():
-            go_right(own).start()
+            go_right(own, h).start()
 
         @pl.when(i > 0)
         def _():
-            go_left(own).start()
-
-        go_x(own).start()
-        go_core(own, col, 0).start()
+            go_left(own, h).start()
+
+        go_x(own, h).start()
+        if h == 1:
+            go_core(own, col, 0).start()
 
     def here(k):
         load(k, micro[0][k], mine_to[k]).wait()
@@ -225,8 +239,13 @@
     here(2)
     values = raw[...].astype(jnp.float32)
     scale = lax.rsqrt(jnp.mean(values * values, axis=-1, keepdims=True) + 1e-06)
-    gain_copy.wait_recv()
-    factor = jnp.where(core == 0, gain[...], gain_in[...])
+
+    @pl.when(core == 1)
+    def _():
+        gain_copy.wait_recv()
+        gain[...] = gain_in[...]
+
+    factor = gain[...]
     data[0] = (values * scale * factor).astype(jnp.bfloat16)
     here(3)
     pack(main, rem, data.reshape(4 * TOK, D), packed)
@@ -234,58 +253,65 @@
     def _():
         keep.start()
         keep.wait()
-        spread_own()
+        spread_own(0)
+        spread_own(1)
 
     @pl.when(core == 1)
     def _():
-        to_mirror.start()
+        for copy in to_mirror:
+            copy.start()
 
     def issue(point):
-        for copy, k in ((to_right, 3 - i), (to_left, i), (to_across, 4 + half * (3 - i) + (1 - half) * i)):
+        for copies, k in ((to_right, 3 - i), (to_left, i), (to_across, 4 + half * (3 - i) + (1 - half) * i)):
             due = (k <= AHEAD) if point == 0 else (k == AHEAD + point)
 
             @pl.when(due)
             def _():
-                copy.start()
+                for copy in copies:
+                    copy.start()
 
     issue(0)
     grad[...] = jnp.zeros_like(grad)
 
     @pl.when(core == 1)
     def _():
-        arrived(own, col)
-        spread_own()
-
-    def from_left(slot):
-        arrived(slot, col)
+        for h in range(2):
+            arrived(own, col, h)
+            spread_own(h)
+
+    def from_left(slot, h):
+        arrived(slot, col, h)
 
         @pl.when(i < 3)
         def _():
-            go_right(slot).start()
-
-        go_x(slot).start()
-        go_core(slot, col, 0).start()
-
-    def from_right(slot):
-        arrived(slot, col)
+            go_right(slot, h).start()
+
+        go_x(slot, h).start()
+        if h == 1:
+            go_core(slot, col, 0).start()
+
+    def from_right(slot, h):
+        arrived(slot, col, h)
 
         @pl.when(i > 0)
         def _():
-            go_left(slot).start()
-
-        go_x(slot).start()
-        go_core(slot, col, 0).start()
+            go_left(slot, h).start()
+
+        go_x(slot, h).start()
+        if h == 1:
+            go_core(slot, col, 0).start()
 
     def from_x(slot):
-        arrived(slot, xcol)
+        arrived(slot, xcol, 0)
+        arrived(slot, xcol, 1)
         go_core(slot, xcol, 1).start()
 
     def compute(base, slots, last=False):
         block = pl.ds(base, slots)
         main, rest = slots * 64, slots * 16
         for k in range(slots):
-            arrived(base + k, x_lo * 2 + 1 - core)
-            arrived(base + k, (1 - x_lo) * 2 + 1 - core)
+            from_core(base + k, x_lo * 2 + 1 - core)
+            from_core(base + k, (1 - x_lo) * 2 + 1 - core)
         out_row, in_row = iota((main, main), 0), iota((main, main), 1)
         source = ((out_row % rest) // 4) * 16 + (out_row // rest) * 4 + out_row % 4
         turn = jnp.where(in_row == source, 1.0, 0.0).astype(jnp.bfloat16)
@@ -339,13 +365,15 @@
 
     for step in range(9):
 
-        @pl.when(step <= 5 + i)
-        def _():
-            from_left(own + 1 + step)
-
-        @pl.when(step <= 8 - i)
-        def _():
-            from_right(own - 1 - step)
+        for h in range(2):
+
+            @pl.when(step <= 5 + i)
+            def _():
+                from_left(own + 1 + step, h)
+
+            @pl.when(step <= 8 - i)
+            def _():
+                from_right(own - 1 - step, h)
 
         issue(step + 1)
         along_x(step - 1)
@@ -360,30 +388,36 @@
     along_x(8)
     compute(14 * half, 2, last=True)
 
+    @pl.when(core == 0)
+    def _():
+        gain_copy.wait_recv()
+
     gain_copy.wait_send()
     for k in range(4):
         swap(k, 0).wait_send()
-    to_right.wait_send()
-    to_left.wait_send()
-    to_across.wait_send()
+    for copy in to_right + to_left + to_across:
+        copy.wait_send()
 
     @pl.when(core == 1)
     def _():
-        to_mirror.wait_send()
+        for copy in to_mirror:
+            copy.wait_send()
 
     for slot in range(16):
-        go_x(slot).wait_send()
         go_core(slot, col, 0).wait_send()
         go_core(slot, xcol, 1).wait_send()
-    for slot in range(16):
+        for h in range(2):
+            go_x(slot, h).wait_send()
 
         @pl.when((slot >= own) & (i < 3))
         def _():
-            go_right(slot).wait_send()
+            for h in range(2):
+                go_right(slot, h).wait_send()
 
         @pl.when((slot <= own) & (i > 0))
         def _():
-            go_left(slot).wait_send()
+            for h in range(2):
+                go_left(slot, h).wait_send()
 
 
 def body(fx, fg, rx, rg, f_routes, r_routes, f_scores, r_scores, gain, w_gate, w_up):
@@ -392,7 +426,7 @@
     return pl.pallas_call(
         kernel,
         name="routed_grad",
-        out_shape=jax.ShapeDtypeStruct((1, HID, D), jnp.bfloat16),
+        out_shape=pltpu.VMEM((1, HID, D), jnp.bfloat16),
         in_specs=[hbm] * 11,
         out_specs=vmem,
         scratch_shapes=[
@@ -401,14 +435,15 @@
             pltpu.VMEM((2, 8, TOK), jnp.float32),
             pltpu.VMEM((1, D), jnp.float32),
             pltpu.VMEM((1, D), jnp.float32),
+            pltpu.VMEM((1, D), jnp.float32),
             pltpu.VMEM((2 * TOK, D), jnp.bfloat16),
             pltpu.VMEM((2, 2 * TOK, D), jnp.bfloat16),
             pltpu.VMEM((4, ROWS, LANES), jnp.bfloat16),
             pltpu.VMEM((D, 2 * HID), jnp.bfloat16),
             pltpu.VMEM((256, LANES), jnp.bfloat16),
             pltpu.VMEM((HID, D), jnp.float32),
-            dma((7,)), dma, dma((2,)), dma((4,)), dma((4,)), dma((4,)), dma((16,)), dma((16,)), dma((16,)),
-            dma((16, 2)), dma((16, 4)),
+            dma((7,)), dma, dma((2,)), dma((4,)), dma((4,)), dma((4, 2)), dma((16, 2)), dma((16, 2)), dma((16, 2)),
+            dma((16, 2)), dma((16, 4, 2)),
         ],
         compiler_params=pltpu.CompilerParams(
             collective_id=0, has_side_effects=True, vmem_limit_bytes=63 << 20

time: 89 us -> 84.7 us (0.952); the launches traced: 87.8 us -> 84.6 us
  Pallas kernels: 85.7 us -> 83.6 us
  local copies, waits for them, and re-layouts: 2.16 us -> 0.93 us
    pallas_call x1, Pallas kernels: 85.7 us -> 83.6 us  [body(): pl.pallas_call(kernel, name='routed_grad', out_shape=pltpu.VMEM((1, HID,...]
    unnamed x1, local copies, waits for them, and re-layouts: 2.16 us -> 0.93 us
where the time goes in v4:
time: 84.7 us; the launch traced here: 84.6 us
  Pallas kernels  83.6 us (99%)
  local copies, waits for them, and re-layouts  0.93 us (1%)
    pallas_call x1, Pallas kernels, body(): pl.pallas_call(kernel, name='routed_grad', out_shape=pltpu.VMEM((1, HID,...  83.6 us

profile of v4, /device:TPU:1, one launch (start us, length us, event | category | flops | bytes accessed | tf_op | source)
XLA Modules:
  0.0 84.6 jit_solution(5175511274929911214)
XLA Ops:
  0.0 83.6 %routed_grad.1 = bf16[1,128,3584]{2,1,0:T(8,128)(2,1)S(1)} custom-call(bf16[1,64,3584]{2,1,0:T(8,128)(2,1)} %fx.1, bf16[1,64,3584]{2,1,0:T(8,128)(2,1)} %fg.1, bf16[1,64,3584]{2,1,0:T(8,128)(2,1)} %rx.1, bf16[1,64,3584]{2,1,0:T(8,128)(2,1)} %rg.1, s32[8,64]{1,0:T(8,128)} %bitcast.12, s32[8,64]{1,0:T(8,128)} %bitcast.13, f32[8,64]{1,0:T(8,128)} %bitcast.14, ...), custom_call_target="tpu_custom_call" | custom-call | flops 6442450944 | bytes 5242880 | tf_op jit(solution)/shard_map/routed_grad/pallas_call | solution.py:426
  83.6 0.9 %copy.13 = bf16[1,128,3584]{2,1,0:T(8,128)(2,1)} copy(bf16[1,128,3584]{2,1,0:T(8,128)(2,1)S(1)} %routed_grad.1) | data formatting | bytes 1835008

commit v5 on v4

--- a/solution.py
+++ b/solution.py
@@ -97,6 +97,37 @@
     z_right = at((z + 1) % 16, x_lo, core)
     z_left = at((z + 15) % 16, x_lo, core)
 
+    barrier = pltpu.get_barrier_semaphore()
+
+    def greet(device):
+        pl.semaphore_signal(barrier, inc=1, device_id=device, device_id_type=MESH)
+
+    greet(core_mate)
+    greet(x_mate)
+    greet(mirror)
+
+    @pl.when(i > 0)
+    def _():
+        greet(z_left)
+
+    @pl.when(i < 3)
+    def _():
+        greet(z_right)
+
+    @pl.when(i == 0)
+    def _():
+        for k in range(4):
+            greet(at(((q + 3) % 4) * 4 + k, far_x, core, far_pipe))
+        for k in (2, 3):
+            greet(at(((q + 2) % 4) * 4 + k, far_x, core, far_pipe))
+
+    @pl.when(i == 3)
+    def _():
+        for k in range(4):
+            greet(at(((q + 1) % 4) * 4 + k, far_x, core, far_pipe))
+        for k in (0, 1):
+            greet(at(((q + 2) % 4) * 4 + k, far_x, core, far_pipe))
+
     def load(k, source, target):
         return pltpu.make_async_copy(source, target, load_sem.at[k])
 
@@ -114,37 +145,6 @@
                 load(k, micro[h][k], mine_to[k]).start()
 
     load_gain.start()
-
-    barrier = pltpu.get_barrier_semaphore()
-
-    def greet(device):
-        pl.semaphore_signal(barrier, inc=1, device_id=device, device_id_type=MESH)
-
-    greet(core_mate)
-    greet(x_mate)
-    greet(mirror)
-
-    @pl.when(i > 0)
-    def _():
-        greet(z_left)
-
-    @pl.when(i < 3)
-    def _():
-        greet(z_right)
-
-    @pl.when(i == 0)
-    def _():
-        for k in range(4):
-            greet(at(((q + 3) % 4) * 4 + k, far_x, core, far_pipe))
-        for k in (2, 3):
-            greet(at(((q + 2) % 4) * 4 + k, far_x, core, far_pipe))
-
-    @pl.when(i == 3)
-    def _():
-        for k in range(4):
-            greet(at(((q + 1) % 4) * 4 + k, far_x, core, far_pipe))
-        for k in (0, 1):
-            greet(at(((q + 2) % 4) * 4 + k, far_x, core, far_pipe))
 
     pl.semaphore_wait(barrier, 7 + (i * (3 - i)) // 2)
 
@@ -318,20 +318,20 @@
         tail = buf[block, :, 64:80, :].reshape(main, LANES)
         spare[:main, :] = jnp.dot(turn, tail, preferred_element_type=jnp.float32).astype(jnp.bfloat16)
 
-        def rows_of(p):
-            return jnp.concatenate(
-                [
-                    buf[block, :, 16 * p : 16 * p + 16, :].reshape(main, LANES),
-                    spare[rest * p : rest * p + rest, :],
-                ],
-                axis=0,
-            )
-
-        both = jnp.zeros((main + rest, 2 * HID), jnp.float32)
-        for p in range(PARTS):
-            both = both + jnp.dot(
-                rows_of(p), weights[p * LANES : (p + 1) * LANES, :], preferred_element_type=jnp.float32
-            )
+        def main_of(p):
+            return buf[block, :, 16 * p : 16 * p + 16, :].reshape(main, LANES)
+
+        def rest_of(p):
+            return spare[rest * p : rest * p + rest, :]
+
+        both = []
+        for size, rows_of in ((main, main_of), (rest, rest_of)):
+            total = jnp.zeros((size, 2 * HID), jnp.float32)
+            for p in range(PARTS):
+                lanes = slice(p * LANES, (p + 1) * LANES)
+                total = total + jnp.dot(rows_of(p), weights[lanes, :], preferred_element_type=jnp.float32)
+            both.append(total)
+        both = jnp.concatenate(both, axis=0)
         gate, up = both[:, :HID], both[:, HID:]
         hidden = gate / (1.0 + jnp.exp(-gate)) * up
         row = iota((main + rest, HID), 0)
@@ -342,7 +342,10 @@
         side = jnp.where(valid, moved, 0.0).T.astype(jnp.bfloat16)
         for p in range(PARTS):
             lanes = slice(p * LANES, (p + 1) * LANES)
-            total = grad[:, lanes] + jnp.dot(side, rows_of(p), preferred_element_type=jnp.float32)
+            total = grad[:, lanes] + jnp.dot(
+                side[:, :main], main_of(p), preferred_element_type=jnp.float32
+            )
+            total = total + jnp.dot(side[:, main:], rest_of(p), preferred_element_type=jnp.float32)
             if last:
                 out_ref[0, :, lanes] = total.astype(jnp.bfloat16)
             else:

time: 84.7 us -> 85 us (level)
  no operation moved by 1% of the time
where the time goes in v5:
time: 85 us; the launch traced here: 84.8 us
  Pallas kernels  83.9 us (99%)
  local copies, waits for them, and re-layouts  0.93 us (1%)
    pallas_call x1, Pallas kernels, body(): pl.pallas_call(kernel, name='routed_grad', out_shape=pltpu.VMEM((1, HID,...  83.9 us

profile of v5, /device:TPU:1, one launch (start us, length us, event | category | flops | bytes accessed | tf_op | source)
XLA Modules:
  0.0 84.8 jit_solution(5435563505098649683)
XLA Ops:
  0.0 83.9 %routed_grad.1 = bf16[1,128,3584]{2,1,0:T(8,128)(2,1)S(1)} custom-call(bf16[1,64,3584]{2,1,0:T(8,128)(2,1)} %fx.1, bf16[1,64,3584]{2,1,0:T(8,128)(2,1)} %fg.1, bf16[1,64,3584]{2,1,0:T(8,128)(2,1)} %rx.1, bf16[1,64,3584]{2,1,0:T(8,128)(2,1)} %rg.1, s32[8,64]{1,0:T(8,128)} %bitcast.12, s32[8,64]{1,0:T(8,128)} %bitcast.13, f32[8,64]{1,0:T(8,128)} %bitcast.14, ...), custom_call_target="tpu_custom_call" | custom-call | flops 6442450944 | bytes 5242880 | tf_op jit(solution)/shard_map/routed_grad/pallas_call | solution.py:429
  83.9 0.9 %copy.13 = bf16[1,128,3584]{2,1,0:T(8,128)(2,1)} copy(bf16[1,128,3584]{2,1,0:T(8,128)(2,1)S(1)} %routed_grad.1) | data formatting | bytes 1835008

commit v6 on v5

--- a/solution.py
+++ b/solution.py
@@ -262,8 +262,11 @@
             copy.start()
 
     def issue(point):
-        for copies, k in ((to_right, 3 - i), (to_left, i), (to_across, 4 + half * (3 - i) + (1 - half) * i)):
-            due = (k <= AHEAD) if point == 0 else (k == AHEAD + point)
+        across = 4 + half * (3 - i) + (1 - half) * i
+        for copies, k, lead in (
+            (to_right, 3 - i, AHEAD), (to_left, i, AHEAD), (to_across, across, 2 * AHEAD)
+        ):
+            due = (k <= lead) if point == 0 else (k == lead + point)
 
             @pl.when(due)
             def _():

time: 85 us -> 85.3 us (level)
  no operation moved by 1% of the time
where the time goes in v6:
time: 85.3 us; the launch traced here: 85.1 us
  Pallas kernels  84.2 us (99%)
  local copies, waits for them, and re-layouts  0.93 us (1%)
    pallas_call x1, Pallas kernels, body(): pl.pallas_call(kernel, name='routed_grad', out_shape=pltpu.VMEM((1, HID,...  84.2 us

profile of v6, /device:TPU:1, one launch (start us, length us, event | category | flops | bytes accessed | tf_op | source)
XLA Modules:
  0.0 85.1 jit_solution(17439140109709648123)
XLA Ops:
  0.0 84.2 %routed_grad.1 = bf16[1,128,3584]{2,1,0:T(8,128)(2,1)S(1)} custom-call(bf16[1,64,3584]{2,1,0:T(8,128)(2,1)} %fx.1, bf16[1,64,3584]{2,1,0:T(8,128)(2,1)} %fg.1, bf16[1,64,3584]{2,1,0:T(8,128)(2,1)} %rx.1, bf16[1,64,3584]{2,1,0:T(8,128)(2,1)} %rg.1, s32[8,64]{1,0:T(8,128)} %bitcast.12, s32[8,64]{1,0:T(8,128)} %bitcast.13, f32[8,64]{1,0:T(8,128)} %bitcast.14, ...), custom_call_target="tpu_custom_call" | custom-call | flops 6442450944 | bytes 5242880 | tf_op jit(solution)/shard_map/routed_grad/pallas_call | solution.py:432
  84.2 0.9 %copy.13 = bf16[1,128,3584]{2,1,0:T(8,128)(2,1)} copy(bf16[1,128,3584]{2,1,0:T(8,128)(2,1)S(1)} %routed_grad.1) | data formatting | bytes 1835008
